TPU v7x, 32 devices: a whole 2x2x4 slice. The times are simulated.
32 devices in a mesh: tm: 4 (over z), space: 8 (over y, x, core).
Axes of the slice: x: 2, y: 2, z: 4, core: 2. Of those that a mesh axis runs over, the one named last changes fastest.
Arguments:
- snaps: bfloat16 [4096, 3, 16384], P('tm', None, 'space')
- phase_bin: int32 [4096], P('tm'), may hold values from 0 to 15, as said below
- owner_order: int32 [16], replicated, may hold values from 0 to 15, each once
- modes: bfloat16 [16, 128, 3, 16384], P(None, None, None, 'space'), may hold values from -0.02734375 to 0.02734375
Outputs:
- phase_mean: bfloat16 [16, 3, 16384], P('tm', None, 'space')
- coefficients: float32 [4096, 128], P('tm')
Inputs may be any that keep to these rules, and one draw needn't show every extreme that they name: `phase_bin`: every bin is named by at least one snapshot; in each aligned block of 1024 snapshots no bin is named more than 128 times.
All inputs are finite; a program needn't handle non-finite values.
Results may differ from a plain program's by a relative error of at most 0.0068.
Values may be sent and summed in bfloat16 or wider, within the bound.
A program may use at most 192 MiB of HBM per device.

v0:
```python
import jax
import jax.numpy as jnp
from jax import lax
from jax.sharding import PartitionSpec as P


def on_device(snaps, phase_bin, owner_order, modes):
    snap_rows = snaps.shape[0]
    cell_count = snaps.shape[2]
    bin_total = modes.shape[0]
    mode_count = modes.shape[1]
    width = 3 * cell_count
    capacity = 2 * snap_rows // bin_total
    flattened = snaps.reshape(snap_rows, width)
    bin_ids = lax.broadcasted_iota(jnp.int32, (bin_total, 1), 0)
    matches = phase_bin[None, :] == bin_ids
    onehot = matches.astype(jnp.bfloat16)
    reorder = (owner_order[:, None] == bin_ids[:, 0][None, :]).astype(jnp.bfloat16)
    chosen = jnp.dot(reorder, onehot, preferred_element_type=jnp.float32)
    chosen_bf = chosen.astype(jnp.bfloat16)
    partial_sums = jnp.dot(chosen_bf, flattened, preferred_element_type=jnp.float32)
    partial_counts = jnp.sum(chosen, axis=1)
    total_sums, total_counts = lax.psum((partial_sums, partial_counts), "tm")
    all_mean = (total_sums / total_counts[:, None]).astype(jnp.bfloat16)
    own_rows = bin_total // lax.axis_size("tm")
    own_mean = lax.dynamic_slice_in_dim(all_mean, lax.axis_index("tm") * own_rows, own_rows, 0)
    phase_mean = own_mean.reshape(own_mean.shape[0], 3, cell_count)
    row_numbers = jnp.arange(bin_total, dtype=jnp.int32)
    inverse = jnp.zeros((bin_total,), jnp.int32).at[owner_order].set(row_numbers)
    mean_by_bin = jnp.take(all_mean, inverse, axis=0)
    match_int = matches.astype(jnp.int32)
    ranks = jnp.cumsum(match_int, axis=1) - 1
    slot = jnp.sum(match_int * ranks, axis=0)
    target = phase_bin * capacity + slot
    snap_numbers = jnp.arange(snap_rows, dtype=jnp.int32)
    source = jnp.full((bin_total * capacity,), snap_rows, jnp.int32).at[target].set(snap_numbers)
    gathered = jnp.take(flattened, source, axis=0, mode="fill", fill_value=0)
    gathered = gathered.reshape(bin_total, capacity, width)
    grouped = (gathered.astype(jnp.float32) - mean_by_bin.astype(jnp.float32)[:, None, :]).astype(
        jnp.bfloat16
    )
    modes_flat = modes.reshape(bin_total, mode_count, width)
    products = lax.dot_general(
        grouped, modes_flat, (((2,), (2,)), ((0,), (0,))), preferred_element_type=jnp.float32
    )
    picked = jnp.take(products.reshape(bin_total * capacity, mode_count), target, axis=0)
    coefficients = lax.psum(picked, "space")
    return (phase_mean, coefficients)


def solution(mesh):
    in_specs = (P("tm", None, "space"), P("tm"), P(), P(None, None, None, "space"))
    out_specs = (P("tm", None, "space"), P("tm", None))
    return jax.shard_map(
        on_device, mesh=mesh, in_specs=in_specs, out_specs=out_specs, check_vma=False
    )
```

profile of v0, /device:TPU:0, one launch (start us, length us, event | category | flops | bytes accessed | tf_op | source)
XLA Modules:
  0.0 239.0 jit_solution(14934051923834580583)
XLA Ops:
  7.2 0.0 copy-start
  7.2 0.0 copy-start.1
  7.2 0.0 all-reduce.3.cloned.1.call-start
  7.2 16.7 %copy.9 = bf16[1024,3,2048]{0,2,1:T(8,128)(2,1)} copy(bf16[1024,3,2048]{2,0,1:T(8,128)(2,1)} %param.4) | data formatting | bytes 25165824 | tf_op args[0]
  23.9 0.0 copy-done
  23.9 0.0 copy-done.1
  23.9 0.3 fusion.17
  24.2 8.7 %fusion.7 = f32[16,6144]{1,0:T(8,128)} fusion(bf16[1024,6144]{0,1:T(8,128)(2,1)} %bitcast.19, bf16[16,1024]{1,0:T(8,128)(2,1)S(1)} %get-tuple-element.5), kind=kOutput, calls=%fused_computation.19 | convolution fusion | flops 201326592 | bytes 13008896 | tf_op jit(solution)/shard_map/dot_general | solution.py:21
  32.9 0.0 all-reduce.3.cloned.1.call-update
  32.9 0.0 all-reduce.5.cloned.1.call-start
  33.0 16.7 %copy.12 = bf16[1024,6144]{1,0:T(8,128)(2,1)} copy(bf16[1024,6144]{0,1:T(8,128)(2,1)} %bitcast.20) | data formatting | bytes 25165824 | tf_op jit(solution)/shard_map/reshape | solution.py:14
  49.7 0.6 scatter_custom_fusion.1
  50.3 13.5 %psum.22 = f32[16]{0:T(128)S(1)} all-reduce(f32[16]{0:T(128)S(1)} %get-tuple-element.4), channel_id=1, replica_groups=mesh['tm'=4,'space'=8] {'tm'}, use_global_device_ids=true, to_apply=%region_2.0 | all-reduce | flops 16 | bytes 128 | tf_op jit(solution)/shard_map/psum | solution.py:23
  63.8 4.5 %reduce-window.6 = s32[16,8,128]{2,1,0:T(8,128)S(1)} reduce-window(s32[16,8,128]{2,1,0:T(8,128)S(1)} %fusion.5, s32[]{:T(128)} %constant.40.clone.1), window={size=1x1x128 pad=0_0x0_0x127_0}, to_apply=%region_3.0 | reduce-window | flops 2080768 | bytes 131076 | tf_op jit(solution)/shard_map/reduce-window
  68.4 0.1 slice.14
  68.4 0.1 copy.10
  68.6 0.1 copy.11
  68.7 0.1 select_reduce_fusion
  68.8 4.5 %scatter_custom_fusion = s32[2048]{0:T(1024)S(1)} fusion(s32[1024]{0:T(1024)S(1)} %get-tuple-element.3, s32[1024]{0:T(1024)S(1)} %iota.22, s32[]{:T(128)} %constant.65.clone.1), kind=kCustom, calls=%fused_computation.29 | custom fusion | bytes 8196 | tf_op jit(solution)/shard_map/scatter | solution.py:36
  73.3 32.6 %copy.13 = bf16[16,128,3,2048]{1,3,2,0:T(8,128)(2,1)} copy(bf16[16,128,3,2048]{3,1,2,0:T(8,128)(2,1)} %param.7) | data formatting | bytes 50331648 | tf_op args[3]
  106.0 48.0 %gather_fusion = bf16[2048,6144]{1,0:T(8,128)(2,1)} fusion(bf16[1024,6144]{1,0:T(8,128)(2,1)} %copy.12, s32[2048]{0:T(1024)S(1)} %fusion.10), kind=kCustom, calls=%fused_computation | custom fusion | bytes 50339840 | tf_op jit(solution)/shard_map/jit(_take)/gather | solution.py:37
  154.0 0.0 all-reduce.3.cloned.1.call-done
  154.0 1.1 divide_convert_fusion
  155.1 0.7 gather_fusion.1
  155.8 0.1 select_convert_fusion
  155.9 17.7 %fusion = f32[16,128,128]{2,1,0:T(8,128)S(1)} fusion(bf16[16,128,6144]{1,2,0:T(8,128)(2,1)} %bitcast.21, f32[16,6144]{1,0:T(8,128)S(1)} %select_convert_fusion, bf16[16,128,6144]{2,1,0:T(8,128)(2,1)} %bitcast.22, pred[16,128]{1,0:T(8,128)(4,1)S(1)} %and_bitcast_fusion), kind=kOutput, calls=%fused_computation.6 | convolution fusion | flops 3271557120 | bytes 51775488 | tf_op jit(solution)/shard_map/dot_general | solution.py:43
  173.6 2.8 %gather_fusion.2 = f32[1024,128]{1,0:T(8,128)S(1)} fusion(f32[2048,128]{1,0:T(8,128)S(1)} %bitcast.23, s32[1024]{0:T(1024)S(1)} %broadcast_clamp_fusion), kind=kCustom, calls=%fused_computation.2 | custom fusion | bytes 1052672 | tf_op jit(solution)/shard_map/jit(_take)/gather | solution.py:46
  176.4 1.0 broadcast_select_fusion
  177.4 0.0 all-reduce.5.cloned.1.call-update
  177.4 0.7 constant_dynamic-slice_fusion
  178.1 52.2 %all-reduce.5.cloned.1.call-done = f32[1024,128]{1,0:T(8,128)} async-done(((f32[1024,128]{1,0:T(8,128)}), f32[1024,128]{1,0:T(8,128)}) %all-reduce.5.cloned.1.call-update) | async-done | bytes 524304 | tf_op jit(solution)/shard_map/psum | solution.py:47
  230.3 1.9 copy.18
  (13 shorter events, 0.1 us)
Async XLA Ops:
  7.2 16.8 %copy-start = (s32[1024]{0:T(1024)S(1)}, s32[1024]{0:T(1024)}, u32[]{:S(2)}) copy-start(s32[1024]{0:T(1024)} %param.5) | copy-start | bytes 12292
  7.2 16.7 %copy-start.1 = (s32[16]{0:T(128)S(1)}, s32[16]{0:T(128)}, u32[]{:S(2)}) copy-start(s32[16]{0:T(128)} %param.6) | copy-start | bytes 196
  7.2 146.8 %all-reduce.3.cloned.1.call-start = ((), (), s32[]{:S(2)}) async-start(), calls=%async_computation | async-start | bytes 786432 | tf_op jit(solution)/shard_map/psum | solution.py:23
  32.9 197.3 %all-reduce.5.cloned.1.call-start = ((), (), s32[]{:S(2)}) async-start(), calls=%async_computation.1 | async-start | bytes 1048576 | tf_op jit(solution)/shard_map/psum | solution.py:47
Sparse Core Ops, SparseCore 0:
  33.1 39.8 all-reduce.2
  177.5 52.6 all-reduce.4
where the time goes:
time: 241 us; the launch traced here: 239 us
  local copies, waits for them, and re-layouts  125 us (52%)
  waiting for transfers between devices  52.2 us (22%)
  matrix products  26.7 us (11%)
  between operations  14.2 us (6%)
  blocking collectives  13.5 us (6%)
  other arithmetic  6.89 us (3%)
    psum x1, waiting for transfers between devices, on_device(): coefficients = lax.psum(picked, 'space')  52.2 us
    unnamed x7, local copies, waits for them, and re-layouts  51.2 us
    gather x1, local copies, waits for them, and re-layouts, on_device(): gathered = jnp.take(flattened, source, axis=0, mode='fill', fill_value=0)  48 us
    dot_general x1, matrix products, on_device(): lax.dot_general(grouped, modes_flat, (((2,), (2,)), ((0,), (0,))), prefer...  17.7 us
    reshape x1, local copies, waits for them, and re-layouts, on_device(): flattened = snaps.reshape(snap_rows, width)  16.7 us
    psum x1, blocking collectives, on_device(): total_sums, total_counts = lax.psum((partial_sums, partial_counts), 'tm')  13.5 us
    dot_general x1, matrix products, on_device(): jnp.dot(chosen_bf, flattened, preferred_element_type=jnp.float32)  8.7 us
  transfers between devices with their start and end apart: 2, of which 1 were waited for; matrix products, arithmetic and copies ran while one was open for 45% of the time, Pallas kernels for 0%

commit v1 on v0

--- a/solution.py
+++ b/solution.py
@@ -44,7 +44,7 @@
         grouped, modes_flat, (((2,), (2,)), ((0,), (0,))), preferred_element_type=jnp.float32
     )
     picked = jnp.take(products.reshape(bin_total * capacity, mode_count), target, axis=0)
-    coefficients = lax.psum(picked, "space")
+    coefficients = jnp.sum(lax.all_gather(picked, "space"), axis=0)
     return (phase_mean, coefficients)
 
 

time: 241 us -> 224 us (0.929)
  waiting for transfers between devices: 52.2 us -> 34.5 us
  other arithmetic: 6.89 us -> 10.1 us
    psum x1 -> x0, waiting for transfers between devices: 52.2 us -> none  [on_device(): coefficients = lax.psum(picked, 'space')]
    all_gather x0 -> x1, waiting for transfers between devices: none -> 34.4 us  [on_device(): coefficients = jnp.sum(lax.all_gather(picked, 'space'), axis=0)]
    reduce_sum x0 -> x1, other arithmetic: none -> 3.24 us  [on_device(): coefficients = jnp.sum(lax.all_gather(picked, 'space'), axis=0)]
    unnamed x7 -> x6, local copies, waits for them, and re-layouts: 51.2 us -> 49.3 us
  transfers between devices with their start and end apart: 2 -> 2, of which waited for: 1 -> 1; matrix products, arithmetic and copies ran while one was open for 45% -> 49% of each run, Pallas kernels for 0% -> 0%
where the time goes in v1:
time: 224 us; the launch traced here: 223 us
  local copies, waits for them, and re-layouts  124 us (55%)
  waiting for transfers between devices  34.5 us (15%)
  matrix products  26.7 us (12%)
  between operations  14.2 us (6%)
  blocking collectives  13.5 us (6%)
  other arithmetic  10.1 us (5%)
    unnamed x6, local copies, waits for them, and re-layouts  49.3 us
    gather x1, local copies, waits for them, and re-layouts, on_device(): gathered = jnp.take(flattened, source, axis=0, mode='fill', fill_value=0)  48 us
    all_gather x1, waiting for transfers between devices, on_device(): coefficients = jnp.sum(lax.all_gather(picked, 'space'), axis=0)  34.4 us
    dot_general x1, matrix products, on_device(): lax.dot_general(grouped, modes_flat, (((2,), (2,)), ((0,), (0,))), prefer...  17.7 us
    reshape x1, local copies, waits for them, and re-layouts, on_device(): flattened = snaps.reshape(snap_rows, width)  16.7 us
    psum x1, blocking collectives, on_device(): total_sums, total_counts = lax.psum((partial_sums, partial_counts), 'tm')  13.5 us
    dot_general x1, matrix products, on_device(): jnp.dot(chosen_bf, flattened, preferred_element_type=jnp.float32)  8.7 us
    another operation x2, other arithmetic  4.55 us
  transfers between devices with their start and end apart: 2, of which 1 were waited for; matrix products, arithmetic and copies ran while one was open for 49% of the time, Pallas kernels for 0%

profile of v1, /device:TPU:0, one launch (start us, length us, event | category | flops | bytes accessed | tf_op | source)
XLA Modules:
  0.0 222.5 jit_solution(3637983912926417796)
XLA Ops:
  7.2 0.0 copy-start
  7.2 0.0 copy-start.1
  7.2 0.0 all-reduce.2.cloned.1.call-start
  7.2 16.7 %copy.15 = bf16[1024,3,2048]{0,2,1:T(8,128)(2,1)} copy(bf16[1024,3,2048]{2,0,1:T(8,128)(2,1)} %param.4) | data formatting | bytes 25165824 | tf_op args[0]
  23.9 0.0 copy-done
  23.9 0.0 copy-done.1
  23.9 0.3 fusion.17
  24.2 8.7 %fusion.7 = f32[16,6144]{1,0:T(8,128)} fusion(bf16[1024,6144]{0,1:T(8,128)(2,1)} %bitcast.21, bf16[16,1024]{1,0:T(8,128)(2,1)S(1)} %get-tuple-element.5), kind=kOutput, calls=%fused_computation.19 | convolution fusion | flops 201326592 | bytes 13008896 | tf_op jit(solution)/shard_map/dot_general | solution.py:21
  32.9 0.0 all-reduce.2.cloned.1.call-update
  32.9 0.0 all-gather.2.cloned.1.call-start
  33.0 16.7 %copy.18 = bf16[1024,6144]{1,0:T(8,128)(2,1)} copy(bf16[1024,6144]{0,1:T(8,128)(2,1)} %bitcast.22) | data formatting | bytes 25165824 | tf_op jit(solution)/shard_map/reshape | solution.py:14
  49.7 0.6 scatter_custom_fusion.1
  50.3 13.5 %psum.15 = f32[16]{0:T(128)S(1)} all-reduce(f32[16]{0:T(128)S(1)} %get-tuple-element.4), channel_id=1, replica_groups=mesh['tm'=4,'space'=8] {'tm'}, use_global_device_ids=true, to_apply=%region_2.0 | all-reduce | flops 16 | bytes 128 | tf_op jit(solution)/shard_map/psum | solution.py:23
  63.8 4.5 %reduce-window.6 = s32[16,8,128]{2,1,0:T(8,128)S(1)} reduce-window(s32[16,8,128]{2,1,0:T(8,128)S(1)} %fusion.5, s32[]{:T(128)} %constant.40.clone.1), window={size=1x1x128 pad=0_0x0_0x127_0}, to_apply=%region_3.0 | reduce-window | flops 2080768 | bytes 131076 | tf_op jit(solution)/shard_map/reduce-window
  68.4 0.1 slice.14
  68.4 0.1 copy.16
  68.6 0.1 copy.17
  68.7 0.1 select_reduce_fusion
  68.8 4.5 %scatter_custom_fusion = s32[2048]{0:T(1024)S(1)} fusion(s32[1024]{0:T(1024)S(1)} %get-tuple-element.3, s32[1024]{0:T(1024)S(1)} %iota.22, s32[]{:T(128)} %constant.65.clone.1), kind=kCustom, calls=%fused_computation.29 | custom fusion | bytes 8196 | tf_op jit(solution)/shard_map/scatter | solution.py:36
  73.3 32.6 %copy.19 = bf16[16,128,3,2048]{1,3,2,0:T(8,128)(2,1)} copy(bf16[16,128,3,2048]{3,1,2,0:T(8,128)(2,1)} %param.7) | data formatting | bytes 50331648 | tf_op args[3]
  105.9 48.0 %gather_fusion = bf16[2048,6144]{1,0:T(8,128)(2,1)} fusion(bf16[1024,6144]{1,0:T(8,128)(2,1)} %copy.18, s32[2048]{0:T(1024)S(1)} %fusion.10), kind=kCustom, calls=%fused_computation | custom fusion | bytes 50339840 | tf_op jit(solution)/shard_map/jit(_take)/gather | solution.py:37
  154.0 0.0 all-reduce.2.cloned.1.call-done
  154.0 1.1 divide_convert_fusion
  155.1 0.7 gather_fusion.1
  155.8 0.1 select_convert_fusion
  155.9 17.7 %fusion = f32[16,128,128]{2,1,0:T(8,128)S(1)} fusion(bf16[16,128,6144]{1,2,0:T(8,128)(2,1)} %bitcast.23, f32[16,6144]{1,0:T(8,128)S(1)} %select_convert_fusion, bf16[16,128,6144]{2,1,0:T(8,128)(2,1)} %bitcast.24, pred[16,128]{1,0:T(8,128)(4,1)S(1)} %and_bitcast_fusion), kind=kOutput, calls=%fused_computation.6 | convolution fusion | flops 3271557120 | bytes 51775488 | tf_op jit(solution)/shard_map/dot_general | solution.py:43
  173.6 2.8 %gather_fusion.2 = f32[1024,128]{1,0:T(8,128)S(1)} fusion(f32[2048,128]{1,0:T(8,128)S(1)} %bitcast.25, s32[1024]{0:T(1024)S(1)} %broadcast_clamp_fusion), kind=kCustom, calls=%fused_computation.2 | custom fusion | bytes 1052672 | tf_op jit(solution)/shard_map/jit(_take)/gather | solution.py:46
  176.4 1.0 bitcast_select_fusion
  177.4 0.0 all-gather.2.cloned.1.call-update
  177.4 0.7 constant_dynamic-slice_fusion
  178.1 34.4 %all-gather.2.cloned.1.call-done = f32[8,1024,128]{2,1,0:T(8,128)} async-done(((f32[1,1024,128]{2,1,0:T(8,128)}), f32[8,1024,128]{2,1,0:T(8,128)}) %all-gather.2.cloned.1.call-update) | async-done | bytes 4194320 | tf_op jit(solution)/shard_map/all_gather | solution.py:47
  212.5 3.2 %reduce_sum.32 = f32[1024,128]{1,0:T(8,128)} reduce(f32[8,1024,128]{2,1,0:T(8,128)} %all-gather.2.cloned.1.call-done, f32[]{:T(128)} %constant.31.clone.1), dimensions={0}, to_apply=%region_8.9 | reduce | flops 917504 | bytes 4718596 | tf_op jit(solution)/shard_map/reduce_sum | solution.py:47
  (13 shorter events, 0.1 us)
Async XLA Ops:
  7.2 16.8 %copy-start = (s32[1024]{0:T(1024)S(1)}, s32[1024]{0:T(1024)}, u32[]{:S(2)}) copy-start(s32[1024]{0:T(1024)} %param.5) | copy-start | bytes 12292
  7.2 16.7 %copy-start.1 = (s32[16]{0:T(128)S(1)}, s32[16]{0:T(128)}, u32[]{:S(2)}) copy-start(s32[16]{0:T(128)} %param.6) | copy-start | bytes 196
  7.2 146.8 %all-reduce.2.cloned.1.call-start = ((), (), s32[]{:S(2)}) async-start(), calls=%async_computation | async-start | bytes 786432 | tf_op jit(solution)/shard_map/psum | solution.py:23
  32.9 179.5 %all-gather.2.cloned.1.call-start = ((), (), s32[]{:S(2)}) async-start(), calls=%async_computation.1 | async-start | bytes 4718592 | tf_op jit(solution)/shard_map/all_gather | solution.py:47
Sparse Core Ops, SparseCore 0:
  33.1 39.8 all-reduce.1
  177.5 34.8 all-gather.1
